TPU v7x, 32 devices: a whole 2x2x4 slice. The times are simulated.
32 devices in a mesh: ctx: 8 (over z, y), fsdp: 4 (over x, core).
Axes of the slice: x: 2, y: 2, z: 4, core: 2. Of those that a mesh axis runs over, the one named last changes fastest.
Arguments:
- normed: bfloat16 [2, 4, 1024, 1024], P(None, 'fsdp', 'ctx'), may hold values from -6 to 6
- out_grad: bfloat16 [2, 4, 1024, 1024], P(None, 'fsdp', 'ctx'), may hold values from -6 to 6
- ids: int32 [2, 4, 1024], P(None, 'fsdp', 'ctx'), may hold values from 0 to 4, as said below
- mask: int32 [2, 4, 1024], P(None, 'fsdp', 'ctx'), may hold values 0 or 1
- proj_half: bfloat16 [512, 1024], P('fsdp'), may hold values from -0.1875 to 0.1875
- conv_filter: float32 [7, 1024], replicated, may hold values from -2.5 to 2.5
- gate_bias: float32 [6, 1024], replicated, may hold values from -6 to 6
Outputs:
- in_grad: bfloat16 [2, 4, 1024, 1024], P(None, 'fsdp', 'ctx')
- proj_grad: float32 [8, 512, 1024], P('ctx', 'fsdp')
- filter_grad: float32 [8, 7, 1024], P('ctx', None, 'fsdp')
- bias_grad: float32 [8, 6, 1024], P('ctx', None, 'fsdp')
Inputs may be any that keep to these rules, and one draw needn't show every extreme that they name: Codes A=0, C=1, G=2, T=3, N=4. ids[1] is the reverse complement of ids[0] in its own coordinates: ids[1, b, p] = 3 - ids[0, b, 1023 - p] where that code is below 4, and 4 where it is 4. Every sequence holds at least one 4.
All inputs are finite; a program needn't handle non-finite values. No bound on the sum of `mask` on one device may be relied on, other than what follows from the above.
Results may differ from a plain program's by a relative error of at most 0.007.
Values may be sent and summed in bfloat16 or wider, within the bound.
A program may use at most 64 MiB of HBM per device.

v0:
```python
import math

import jax
import jax.numpy as jnp
from jax import lax
from jax.sharding import PartitionSpec as P


def from_partner(value, axis, stride):
    mask = 2**stride
    pairs = [(source, source ^ mask) for source in range(lax.axis_size(axis))]
    return lax.ppermute(value, axis, pairs)


def shifted_2(block, axis, distance):
    devices = range(lax.axis_size(axis))
    route = [(i - distance, i) for i in devices if i - distance in devices]
    return lax.ppermute(block, axis, route)


def mirror_slab(slab_in):
    depth_count = lax.axis_size("ctx").bit_length() - 1
    bit_order = list(range(depth_count))
    arrived = slab_in
    for bit_number in bit_order:
        arrived = from_partner(arrived, "ctx", bit_number)
    return jnp.flip(arrived, axis=(0, 2, 3))


def project(rows_in, weight_full):
    return jnp.dot(rows_in, weight_full, preferred_element_type=jnp.float32)


def shards(normed, out_grad, ids, mask, proj_half, conv_filter, gate_bias):
    seq_local = normed.shape[1]
    row_count = normed.shape[2]
    feature_width = normed.shape[3]
    tap_count = conv_filter.shape[0]
    rim_rows = tap_count - 1
    half_rows = lax.all_gather(proj_half, "fsdp", axis=0, tiled=True)
    weight_full = jnp.concatenate([half_rows, jnp.flip(half_rows, axis=(0, 1))], axis=0)
    flat_in = normed.reshape(-1, feature_width)
    mirrored_in = mirror_slab(normed)
    values = project(flat_in, weight_full).astype(jnp.bfloat16).reshape(normed.shape)
    mirrored = (
        project(mirrored_in.reshape(-1, feature_width), weight_full)
        .astype(jnp.bfloat16)
        .reshape(normed.shape)
    )
    before = shifted_2(values[:, :, row_count - rim_rows :, :], "ctx", 1)
    extended = jnp.concatenate([before, values], axis=2)
    conv_out = jnp.zeros(normed.shape, jnp.float32)
    for tap_index in range(tap_count):
        start_row = rim_rows - tap_index
        conv_out = conv_out + conv_filter[tap_index] * extended[
            :, :, start_row : start_row + row_count, :
        ].astype(jnp.float32)
    tokens = jnp.where(mask == 1, 5, ids)
    classes = lax.broadcasted_iota(jnp.int32, (1, 6), 1)
    one_hot = (tokens.reshape(-1, 1) == classes).astype(jnp.float32)
    bias_rows = jnp.dot(one_hot, gate_bias, precision=lax.Precision.HIGHEST).reshape(normed.shape)
    gate = jax.nn.sigmoid(mirrored.astype(jnp.float32) + bias_rows)
    cotangent = out_grad.astype(jnp.float32)
    conv_grad = cotangent * gate
    gate_pre = cotangent * conv_out * gate * (1.0 - gate)
    mirror_grad = gate_pre.astype(jnp.bfloat16)
    following = shifted_2(conv_grad[:, :, :rim_rows, :], "ctx", -1)
    grad_ext = jnp.concatenate([conv_grad, following], axis=2)
    returned = mirror_slab(mirror_grad)
    value_grad = returned.astype(jnp.float32)
    for tap_index in range(tap_count):
        value_grad = (
            value_grad
            + conv_filter[tap_index] * grad_ext[:, :, tap_index : tap_index + row_count, :]
        )
    value_grad = value_grad.astype(jnp.bfloat16)
    flat_grad = value_grad.reshape(-1, feature_width)
    in_grad = lax.dot_general(
        flat_grad, weight_full, (((1,), (1,)), ((), ())), preferred_element_type=jnp.float32
    )
    in_grad = in_grad.astype(jnp.bfloat16).reshape(normed.shape)
    half_width = feature_width // 2
    lower_in = flat_in[:, :half_width]
    upper_in = jnp.flip(flat_in[:, half_width:], axis=1)
    proj_term = lax.dot_general(
        lower_in, flat_grad, (((0,), (0,)), ((), ())), preferred_element_type=jnp.float32
    )
    proj_term = proj_term + lax.dot_general(
        upper_in,
        jnp.flip(flat_grad, axis=1),
        (((0,), (0,)), ((), ())),
        preferred_element_type=jnp.float32,
    )
    filter_terms = []
    for tap_index in range(tap_count):
        start_row = rim_rows - tap_index
        shifted = extended[:, :, start_row : start_row + row_count, :].astype(jnp.float32)
        filter_terms.append(jnp.sum(conv_grad * shifted, axis=(0, 1, 2)))
    filter_term = jnp.stack(filter_terms, axis=0)
    bias_term = lax.dot_general(
        one_hot,
        gate_pre.reshape(-1, feature_width),
        (((0,), (0,)), ((), ())),
        precision=lax.Precision.HIGHEST,
    )
    grad_scale = 1.0 / math.sqrt(2.0 * seq_local * lax.axis_size("fsdp") * row_count)
    proj_sum, filter_sum, bias_sum = (
        lax.psum_scatter(proj_term * grad_scale, "fsdp", scatter_dimension=0, tiled=True),
        lax.psum_scatter(filter_term * grad_scale, "fsdp", scatter_dimension=1, tiled=True),
        lax.psum_scatter(bias_term * grad_scale, "fsdp", scatter_dimension=1, tiled=True),
    )
    return (in_grad, proj_sum[None], filter_sum[None], bias_sum[None])


def solution(mesh):
    placed = (
        P(None, "fsdp", "ctx", None),
        P(None, "fsdp", "ctx", None),
        P(None, "fsdp", "ctx"),
        P(None, "fsdp", "ctx"),
        P("fsdp", None),
        P(),
        P(),
    )
    return jax.shard_map(
        shards,
        mesh=mesh,
        in_specs=placed,
        out_specs=(
            P(None, "fsdp", "ctx", None),
            P("ctx", "fsdp", None),
            P("ctx", None, "fsdp"),
            P("ctx", None, "fsdp"),
        ),
        check_vma=False,
    )
```

profile of v0, /device:TPU:0, one launch (start us, length us, event | category | flops | bytes accessed | tf_op | source)
XLA Modules:
  0.0 203.6 jit_solution(15695145438317743831)
XLA Ops:
  7.2 0.0 all-gather.2.cloned.1.call-start
  7.2 3.0 %collective-permute-start.1 = (bf16[2,1,128,1024]{3,2,1,0:T(8,128)(2,1)}, bf16[2,1,128,1024]{3,2,1,0:T(8,128)(2,1)S(1)}, u32[]{:S(2)}, u32[]{:S(2)}) collective-permute-start(bf16[2,1,128,1024]{3,2,1,0:T(8,128)(2,1)} %param.7), channel_id=1, source_target_pairs={{0,4},{4,0},{8,12},{12,8},{16,20},{20,16},{24,28},{28,24},{1,5},{5... | collective-permute-start | bytes 1572872 | tf_op jit(solution)/shard_map/ppermute | solution.py:12
  10.3 0.0 all-gather.2.cloned.1.call-update
  10.3 0.0 reduce-scatter.8.cloned.1.call-start
  10.3 12.1 %collective-permute-done.1 = bf16[2,1,128,1024]{3,2,1,0:T(8,128)(2,1)S(1)} collective-permute-done((bf16[2,1,128,1024]{3,2,1,0:T(8,128)(2,1)}, bf16[2,1,128,1024]{3,2,1,0:T(8,128)(2,1)S(1)}, u32[]{:S(2)}, u32[]{:S(2)}) %collective-permute-start.1) | collective-permute-done | bytes 524320 | tf_op jit(solution)/shard_map/ppermute | solution.py:12
  22.4 1.8 collective-permute-start.2
  24.2 11.3 %collective-permute-done.2 = bf16[2,1,128,1024]{3,2,1,0:T(8,128)(2,1)S(1)} collective-permute-done((bf16[2,1,128,1024]{3,2,1,0:T(8,128)(2,1)S(1)}, bf16[2,1,128,1024]{3,2,1,0:T(8,128)(2,1)S(1)}, u32[]{:S(2)}, u32[]{:S(2)}) %collective-permute-start.2) | collective-permute-done | bytes 524320 | tf_op jit(solution)/shard_map/ppermute | solution.py:12
  35.5 2.5 %collective-permute-start.3 = (bf16[2,1,128,1024]{3,2,1,0:T(8,128)(2,1)S(1)}, bf16[2,1,128,1024]{3,2,1,0:T(8,128)(2,1)S(1)}, u32[]{:S(2)}, u32[]{:S(2)}) collective-permute-start(bf16[2,1,128,1024]{3,2,1,0:T(8,128)(2,1)S(1)} %collective-permute-done.2), channel_id=1, source_target_pairs={{0,16},{4,20},{8,24},{12,28},{16,0},{20,4},{24,8},{28,12},{1,17},{... | collective-permute-start | bytes 1572872 | tf_op jit(solution)/shard_map/ppermute | solution.py:12
  38.0 0.7 compare_select_fusion
  38.7 1.0 fusion.53
  39.7 20.1 %collective-permute-done.3 = bf16[2,1,128,1024]{3,2,1,0:T(8,128)(2,1)S(1)} collective-permute-done((bf16[2,1,128,1024]{3,2,1,0:T(8,128)(2,1)S(1)}, bf16[2,1,128,1024]{3,2,1,0:T(8,128)(2,1)S(1)}, u32[]{:S(2)}, u32[]{:S(2)}) %collective-permute-start.3) | collective-permute-done | bytes 524320 | tf_op jit(solution)/shard_map/ppermute | solution.py:12
  59.8 1.8 rev.20
  61.6 0.0 all-gather.2.cloned.1.call-done
  61.7 14.0 %rev.19 = bf16[512,1024]{1,0:T(8,128)(2,1)S(1)} reverse(bf16[512,1024]{1,0:T(8,128)(2,1)} %all-gather.2.cloned.1.call-done), dimensions={0,1} | reverse | bytes 2097152 | tf_op jit(solution)/shard_map/jit(_flip)/rev | solution.py:41
  75.7 2.1 %convolution_convert_fusion.1 = bf16[1024,256]{0,1:T(8,128)(2,1)S(1)} fusion(bf16[256,1024]{1,0:T(8,128)(2,1)} %bitcast.60, bf16[512,1024]{1,0:T(8,128)(2,1)S(1)} %rev.19, bf16[512,1024]{1,0:T(8,128)(2,1)S(1)} %copy-done.3), kind=kOutput, calls=%fused_computation.34 | convolution fusion | flops 541327360 | bytes 3145728 | tf_op jit(solution)/shard_map/dot_general | solution.py:31
  77.8 3.0 %collective-permute-start = (bf16[2,1,6,1024]{3,2,1,0:T(8,128)(2,1)S(1)}, bf16[2,1,6,1024]{3,2,1,0:T(8,128)(2,1)S(1)}, u32[]{:S(2)}, u32[]{:S(2)}) collective-permute-start(bf16[2,1,6,1024]{3,2,1,0:T(8,128)(2,1)S(1)} %slice.105), channel_id=1, source_target_pairs={{0,4},{4,8},{8,12},{12,16},{16,20},{20,24},{24,28},{1,5},{5,9},{9,... | collective-permute-start | bytes 73736 | tf_op jit(solution)/shard_map/ppermute | solution.py:18
  80.8 0.7 fusion.5
  81.6 0.8 fusion.3
  82.4 0.0 collective-permute-done
  82.4 0.2 copy-done.2
  82.6 2.1 %fusion.51 = (bf16[2,1,128,1024]{3,2,1,0:T(8,128)(2,1)S(1)}, f32[2,1,128,1024]{3,2,1,0:T(8,128)}) fusion(f32[2,1,128,1024]{3,2,1,0:T(8,128)S(1)} %bitcast.56, bf16[2,1,128,1024]{3,2,1,0:T(8,128)(2,1)S(1)} %bitcast.51, bf16[2,1,6,1024]{3,2,1,0:T(8,128)(2,1)S(1)} %collective-permute-done, f32[1024]{0:T(1024)S(1)} %bitcast.73, f32[1024]{0:T(1024)S(1)} %bitcast.75, ...), kind=kLoop, calls=%fused_computation.92 | loop fusion | flops 11534336 | bytes 3723264 | tf_op jit(solution)/shard_map/convert_element_type | solution.py:66
  84.7 2.1 %collective-permute-start.4 = (bf16[2,1,128,1024]{3,2,1,0:T(8,128)(2,1)S(1)}, bf16[2,1,128,1024]{3,2,1,0:T(8,128)(2,1)}, u32[]{:S(2)}, u32[]{:S(2)}) collective-permute-start(bf16[2,1,128,1024]{3,2,1,0:T(8,128)(2,1)S(1)} %get-tuple-element.16), channel_id=1, source_target_pairs={{0,4},{4,0},{8,12},{12,8},{16,20},{20,16},{24,28},{28,24},{1,5},{5... | collective-permute-start | bytes 1572872 | tf_op jit(solution)/shard_map/ppermute | solution.py:12
  86.8 10.5 %collective-permute-done.4 = bf16[2,1,128,1024]{3,2,1,0:T(8,128)(2,1)} collective-permute-done((bf16[2,1,128,1024]{3,2,1,0:T(8,128)(2,1)S(1)}, bf16[2,1,128,1024]{3,2,1,0:T(8,128)(2,1)}, u32[]{:S(2)}, u32[]{:S(2)}) %collective-permute-start.4) | collective-permute-done | bytes 524320 | tf_op jit(solution)/shard_map/ppermute | solution.py:12
  97.3 2.4 %collective-permute-start.5 = (bf16[2,1,128,1024]{3,2,1,0:T(8,128)(2,1)}, bf16[2,1,128,1024]{3,2,1,0:T(8,128)(2,1)}, u32[]{:S(2)}, u32[]{:S(2)}) collective-permute-start(bf16[2,1,128,1024]{3,2,1,0:T(8,128)(2,1)} %collective-permute-done.4), channel_id=1, source_target_pairs={{0,8},{4,12},{8,0},{12,4},{16,24},{20,28},{24,16},{28,20},{1,9},{5... | collective-permute-start | bytes 1572872 | tf_op jit(solution)/shard_map/ppermute | solution.py:12
  99.7 0.8 rev.23
  100.6 9.5 %collective-permute-done.5 = bf16[2,1,128,1024]{3,2,1,0:T(8,128)(2,1)} collective-permute-done((bf16[2,1,128,1024]{3,2,1,0:T(8,128)(2,1)}, bf16[2,1,128,1024]{3,2,1,0:T(8,128)(2,1)}, u32[]{:S(2)}, u32[]{:S(2)}) %collective-permute-start.5) | collective-permute-done | bytes 524320 | tf_op jit(solution)/shard_map/ppermute | solution.py:12
  110.0 4.5 %collective-permute-start.6 = (bf16[2,1,128,1024]{3,2,1,0:T(8,128)(2,1)}, bf16[2,1,128,1024]{3,2,1,0:T(8,128)(2,1)}, u32[]{:S(2)}, u32[]{:S(2)}) collective-permute-start(bf16[2,1,128,1024]{3,2,1,0:T(8,128)(2,1)} %collective-permute-done.5), channel_id=1, source_target_pairs={{0,16},{4,20},{8,24},{12,28},{16,0},{20,4},{24,8},{28,12},{1,17},{... | collective-permute-start | bytes 1572872 | tf_op jit(solution)/shard_map/ppermute | solution.py:12
  114.5 1.1 fusion.20
  115.6 1.3 collective-permute-start.7
  117.0 1.1 convolution_multiply_fusion
  118.1 0.0 reduce-scatter.8.cloned.1.call-update
  118.1 0.0 reduce-scatter.6.cloned.1.call-start
  118.2 0.1 stack.31
  118.2 0.6 broadcast_multiply_fusion
  118.9 0.0 reduce-scatter.4.cloned.1.call-start
  118.9 17.1 %collective-permute-done.6 = bf16[2,1,128,1024]{3,2,1,0:T(8,128)(2,1)} collective-permute-done((bf16[2,1,128,1024]{3,2,1,0:T(8,128)(2,1)}, bf16[2,1,128,1024]{3,2,1,0:T(8,128)(2,1)}, u32[]{:S(2)}, u32[]{:S(2)}) %collective-permute-start.6) | collective-permute-done | bytes 524320 | tf_op jit(solution)/shard_map/ppermute | solution.py:12
  136.0 7.0 %rev.21 = bf16[2,1,128,1024]{3,2,1,0:T(8,128)(2,1)S(1)} reverse(bf16[2,1,128,1024]{3,2,1,0:T(8,128)(2,1)} %collective-permute-done.6), dimensions={0,2,3} | reverse | bytes 1048576 | tf_op jit(solution)/shard_map/jit(_flip)/rev | solution.py:27
  143.0 1.0 fusion.25
  144.0 0.5 fusion.44
  144.5 1.7 rev.22
  146.2 1.8 multiply_bitcast_fusion
  148.0 0.0 reduce-scatter.8.cloned.1.call-done
  148.1 1.4 copy.19
  149.5 11.8 %reduce-scatter.6.cloned.1.call-done = f32[7,256]{1,0:T(8,128)} async-done(((f32[7,1024]{1,0:T(8,128)}), f32[7,256]{1,0:T(8,128)}) %reduce-scatter.6.cloned.1.call-update) | async-done | bytes 7184 | tf_op jit(solution)/shard_map/reduce_scatter | solution.py:109
  161.3 1.3 broadcast_in_dim.15
  162.6 1.5 convolution_convert_fusion.2
  164.1 31.0 %reduce-scatter.4.cloned.1.call-done = f32[128,1024]{0,1:T(8,128)} async-done(((f32[512,1024]{0,1:T(8,128)}), f32[128,1024]{0,1:T(8,128)}) %reduce-scatter.4.cloned.1.call-update) | async-done | bytes 524304 | tf_op jit(solution)/shard_map/reduce_scatter | solution.py:108
  195.1 2.0 copy.18
  (23 shorter events, 0.1 us)
Async XLA Ops:
  7.2 74.4 %copy-start = (f32[6,1024]{1,0:T(8,128)S(1)}, f32[6,1024]{1,0:T(8,128)}, u32[]{:S(2)}) copy-start(f32[6,1024]{1,0:T(8,128)} %param.13) | copy-start | bytes 73732
  7.2 54.5 %all-gather.2.cloned.1.call-start = ((), (), s32[]{:S(2)}) async-start(), calls=%async_computation.3 | async-start | bytes 1310720 | tf_op jit(solution)/shard_map/all_gather | solution.py:40
  7.2 15.2 %collective-permute-start.1 = (bf16[2,1,128,1024]{3,2,1,0:T(8,128)(2,1)}, bf16[2,1,128,1024]{3,2,1,0:T(8,128)(2,1)S(1)}, u32[]{:S(2)}, u32[]{:S(2)}) collective-permute-start(bf16[2,1,128,1024]{3,2,1,0:T(8,128)(2,1)} %param.7), channel_id=1, source_target_pairs={{0,4},{4,0},{8,12},{12,8},{16,20},{20,16},{24,28},{28,24},{1,5},{5... | collective-permute-start | bytes 1572872 | tf_op jit(solution)/shard_map/ppermute | solution.py:12
  10.3 137.8 %reduce-scatter.8.cloned.1.call-start = ((), (), s32[]{:S(2)}) async-start(), calls=%async_computation.6 | async-start | bytes 40960 | tf_op jit(solution)/shard_map/reduce_scatter | solution.py:110
  22.4 13.1 %collective-permute-start.2 = (bf16[2,1,128,1024]{3,2,1,0:T(8,128)(2,1)S(1)}, bf16[2,1,128,1024]{3,2,1,0:T(8,128)(2,1)S(1)}, u32[]{:S(2)}, u32[]{:S(2)}) collective-permute-start(bf16[2,1,128,1024]{3,2,1,0:T(8,128)(2,1)S(1)} %collective-permute-done.1), channel_id=1, source_target_pairs={{0,8},{4,12},{8,0},{12,4},{16,24},{20,28},{24,16},{28,20},{1,9},{5... | collective-permute-start | bytes 1572872 | tf_op jit(solution)/shard_map/ppermute | solution.py:12
  35.5 24.3 %collective-permute-start.3 = (bf16[2,1,128,1024]{3,2,1,0:T(8,128)(2,1)S(1)}, bf16[2,1,128,1024]{3,2,1,0:T(8,128)(2,1)S(1)}, u32[]{:S(2)}, u32[]{:S(2)}) collective-permute-start(bf16[2,1,128,1024]{3,2,1,0:T(8,128)(2,1)S(1)} %collective-permute-done.2), channel_id=1, source_target_pairs={{0,16},{4,20},{8,24},{12,28},{16,0},{20,4},{24,8},{28,12},{1,17},{... | collective-permute-start | bytes 1572872 | tf_op jit(solution)/shard_map/ppermute | solution.py:12
  61.7 14.0 %copy-start.3 = (bf16[512,1024]{1,0:T(8,128)(2,1)S(1)}, bf16[512,1024]{1,0:T(8,128)(2,1)}, u32[]{:S(2)}) copy-start(bf16[512,1024]{1,0:T(8,128)(2,1)} %all-gather.2.cloned.1.call-done) | copy-start | bytes 3145732
  75.6 5.2 %copy-start.5 = (bf16[512,1024]{1,0:T(8,128)(2,1)}, bf16[512,1024]{1,0:T(8,128)(2,1)S(1)}, u32[]{:S(2)}) copy-start(bf16[512,1024]{1,0:T(8,128)(2,1)S(1)} %rev.19) | copy-start | bytes 3145732
  77.8 4.6 %collective-permute-start = (bf16[2,1,6,1024]{3,2,1,0:T(8,128)(2,1)S(1)}, bf16[2,1,6,1024]{3,2,1,0:T(8,128)(2,1)S(1)}, u32[]{:S(2)}, u32[]{:S(2)}) collective-permute-start(bf16[2,1,6,1024]{3,2,1,0:T(8,128)(2,1)S(1)} %slice.105), channel_id=1, source_target_pairs={{0,4},{4,8},{8,12},{12,16},{16,20},{20,24},{24,28},{1,5},{5,9},{9,... | collective-permute-start | bytes 73736 | tf_op jit(solution)/shard_map/ppermute | solution.py:18
  81.6 1.0 copy-start.2
  82.4 17.3 %copy-start.7 = (bf16[2,1,128,1024]{3,2,1,0:T(8,128)(2,1)S(1)}, bf16[2,1,128,1024]{3,2,1,0:T(8,128)(2,1)}, u32[]{:S(2)}) copy-start(bf16[2,1,128,1024]{3,2,1,0:T(8,128)(2,1)} %param.7) | copy-start | bytes 1572868
  84.7 12.6 %collective-permute-start.4 = (bf16[2,1,128,1024]{3,2,1,0:T(8,128)(2,1)S(1)}, bf16[2,1,128,1024]{3,2,1,0:T(8,128)(2,1)}, u32[]{:S(2)}, u32[]{:S(2)}) collective-permute-start(bf16[2,1,128,1024]{3,2,1,0:T(8,128)(2,1)S(1)} %get-tuple-element.16), channel_id=1, source_target_pairs={{0,4},{4,0},{8,12},{12,8},{16,20},{20,16},{24,28},{28,24},{1,5},{5... | collective-permute-start | bytes 1572872 | tf_op jit(solution)/shard_map/ppermute | solution.py:12
  97.3 12.7 %collective-permute-start.5 = (bf16[2,1,128,1024]{3,2,1,0:T(8,128)(2,1)}, bf16[2,1,128,1024]{3,2,1,0:T(8,128)(2,1)}, u32[]{:S(2)}, u32[]{:S(2)}) collective-permute-start(bf16[2,1,128,1024]{3,2,1,0:T(8,128)(2,1)} %collective-permute-done.4), channel_id=1, source_target_pairs={{0,8},{4,12},{8,0},{12,4},{16,24},{20,28},{24,16},{28,20},{1,9},{5... | collective-permute-start | bytes 1572872 | tf_op jit(solution)/shard_map/ppermute | solution.py:12
  100.5 16.4 %copy-start.1 = (f32[2,1,128,1024]{3,2,1,0:T(8,128)S(1)}, f32[2,1,128,1024]{3,2,1,0:T(8,128)}, u32[]{:S(2)}) copy-start(f32[2,1,128,1024]{3,2,1,0:T(8,128)} %get-tuple-element.17) | copy-start | bytes 3145732
  110.0 26.0 %collective-permute-start.6 = (bf16[2,1,128,1024]{3,2,1,0:T(8,128)(2,1)}, bf16[2,1,128,1024]{3,2,1,0:T(8,128)(2,1)}, u32[]{:S(2)}, u32[]{:S(2)}) collective-permute-start(bf16[2,1,128,1024]{3,2,1,0:T(8,128)(2,1)} %collective-permute-done.5), channel_id=1, source_target_pairs={{0,16},{4,20},{8,24},{12,28},{16,0},{20,4},{24,8},{28,12},{1,17},{... | collective-permute-start | bytes 1572872 | tf_op jit(solution)/shard_map/ppermute | solution.py:12
  115.6 27.4 %collective-permute-start.7 = (f32[2,1,6,1024]{3,2,1,0:T(8,128)S(1)}, f32[2,1,6,1024]{3,2,1,0:T(8,128)S(1)}, u32[]{:S(2)}, u32[]{:S(2)}) collective-permute-start(f32[2,1,6,1024]{3,2,1,0:T(8,128)S(1)} %slice.116), channel_id=1, source_target_pairs={{4,0},{8,4},{12,8},{16,12},{20,16},{24,20},{28,24},{5,1},{9,5},{13... | collective-permute-start | bytes 147464 | tf_op jit(solution)/shard_map/ppermute | solution.py:18
  117.0 27.1 %copy-start.8 = (bf16[2,1,128,1024]{3,2,1,0:T(8,128)(2,1)S(1)}, bf16[2,1,128,1024]{3,2,1,0:T(8,128)(2,1)}, u32[]{:S(2)}) copy-start(bf16[2,1,128,1024]{3,2,1,0:T(8,128)(2,1)} %param.7) | copy-start | bytes 1572868
  118.1 43.1 %reduce-scatter.6.cloned.1.call-start = ((), (), s32[]{:S(2)}) async-start(), calls=%async_computation.5 | async-start | bytes 40960 | tf_op jit(solution)/shard_map/reduce_scatter | solution.py:109
  118.9 76.2 %reduce-scatter.4.cloned.1.call-start = ((), (), s32[]{:S(2)}) async-start(), calls=%async_computation.4 | async-start | bytes 2621440 | tf_op jit(solution)/shard_map/reduce_scatter | solution.py:108
  148.0 14.6 %copy-start.4 = (bf16[512,1024]{1,0:T(8,128)(2,1)S(1)}, bf16[512,1024]{1,0:T(8,128)(2,1)}, u32[]{:S(2)}) copy-start(bf16[512,1024]{1,0:T(8,128)(2,1)} %all-gather.2.cloned.1.call-done) | copy-start | bytes 3145732
  148.0 14.6 %copy-start.6 = (bf16[512,1024]{1,0:T(8,128)(2,1)S(1)}, bf16[512,1024]{1,0:T(8,128)(2,1)}, u32[]{:S(2)}) copy-start(bf16[512,1024]{1,0:T(8,128)(2,1)} %copy-done.5) | copy-start | bytes 3145732
Sparse Core Ops, SparseCore 0:
  10.4 18.5 all-gather.1
  118.2 20.4 reduce-scatter.7
  141.9 19.3 reduce-scatter.5
  163.6 31.3 reduce-scatter.3
where the time goes:
time: 206 us; the launch traced here: 204 us
  waiting for transfers between devices  123 us (60%)
  local copies, waits for them, and re-layouts  31.4 us (15%)
  starting transfers between devices  20.7 us (10%)
  between operations  14 us (7%)
  matrix products  8.54 us (4%)
  other arithmetic  5.54 us (3%)
    ppermute x6, waiting for transfers between devices, from_partner(): return lax.ppermute(value, axis, pairs)  80.5 us
    reduce_scatter x1, waiting for transfers between devices, shards(): lax.psum_scatter(proj_term * grad_scale, 'fsdp', scatter_dimension=0, til...  31 us
    ppermute x6, starting transfers between devices, from_partner(): return lax.ppermute(value, axis, pairs)  16.3 us
    rev x1, local copies, waits for them, and re-layouts, shards(): jnp.flip(half_rows, axis=(0, 1))  14 us
    reduce_scatter x1, waiting for transfers between devices, shards(): lax.psum_scatter(filter_term * grad_scale, 'fsdp', scatter_dimension=1, t...  11.8 us
    rev x2, local copies, waits for them, and re-layouts, mirror_slab(): return jnp.flip(arrived, axis=(0, 2, 3))  8.8 us
    ppermute x2, starting transfers between devices, shifted_2(): return lax.ppermute(block, axis, route)  4.3 us
  transfers between devices with their start and end apart: 12, of which 8 were waited for; matrix products, arithmetic and copies ran while one was open for 12% of the time, Pallas kernels for 0%

commit v1 on v0

v1 whole, which is shorter than its diff:
```python
import functools
import math

import jax
import jax.numpy as jnp
from jax import lax
from jax.experimental import pallas as pl
from jax.experimental.pallas import tpu as pltpu
from jax.sharding import PartitionSpec as P

MESH = pl.DeviceIdType.MESH
BF = jnp.bfloat16
F32 = jnp.float32
PAD = 8


def mm(a, b):
    return jnp.dot(a, b, preferred_element_type=F32)


def mm_nt(a, b):
    return lax.dot_general(a, b, (((1,), (1,)), ((), ())), preferred_element_type=F32)


def anti(size):
    row = lax.broadcasted_iota(jnp.int32, (size, size), 0)
    col = lax.broadcasted_iota(jnp.int32, (size, size), 1)
    return jnp.where(row + col == size - 1, 1.0, 0.0).astype(BF)


def eye(size):
    row = lax.broadcasted_iota(jnp.int32, (size, size), 0)
    col = lax.broadcasted_iota(jnp.int32, (size, size), 1)
    return jnp.where(row == col, 1.0, 0.0).astype(BF)


def split3(x):
    hi = x.astype(BF)
    rest = x - hi.astype(F32)
    mid = rest.astype(BF)
    low = (rest - mid.astype(F32)).astype(BF)
    return hi, mid, low


def flip_f32(x, j):
    hi, mid, low = split3(x)
    return (mm(hi, j) + mm(mid, j)) + mm(low, j)


def kernel(
    n, nf, taps, scale,
    n_ref, g_ref, ids_ref, mask_ref, proj_ref, filt_ref, bias_ref,
    in_out, proj_out, filt_out, bias_out,
    m_s, m_r, g1s, g1r, vgs, vgr, vg0, hs, hr, toks, tokr, w, v0, v1, cg0s, cg1s,
    gh0, gh1, oh, oht, gb, ft, fb, s0, s1, sr, at, pf, cs, cr, xs, xr,
    m_sem, g_sem, vg_sem, h_sem, t_sem, w_sem, wf_sem, s0_sem, s1_sem, c_sem, x_sem,
):
    rows, width = m_s.shape
    nc, _, cw = g1s.shape
    nx = nf // 2
    half = width // 2
    c = lax.axis_index("ctx")
    f = lax.axis_index("fsdp")
    core, chip = lax.rem(f, 2), f // 2
    sib = chip * 2 + 1 - core
    partner = n - 1 - c
    up, down = lax.rem(c + 1, n), lax.rem(c + n - 1, n)
    t_prev = lax.rem(2 * n - 2 - c, n)
    t_next = lax.rem(n - c, n)

    def rdma(src, dst, sems, cc, ff):
        return pltpu.make_async_remote_copy(
            src_ref=src, dst_ref=dst, send_sem=sems.at[0], recv_sem=sems.at[1],
            device_id=(cc, ff), device_id_type=MESH,
        )

    barrier = pltpu.get_barrier_semaphore()

    def greet(cc, ff):
        pl.semaphore_signal(barrier, inc=1, device_id=(cc, ff), device_id_type=MESH)

    for t in range(nf):
        greet(partner, lax.rem(f + t, nf))
    for t in range(1, nf):
        greet(c, lax.rem(f + t, nf))
    greet(up, f)
    greet(down, f)
    for target in (t_prev, t_next):
        @pl.when(target != c)
        def _():
            greet(target, f)

    jr = anti(rows)
    jc = anti(cw)

    def flip_cols(x):
        parts = [mm(x[:, q * cw : (q + 1) * cw], jc).astype(BF) for q in reversed(range(nc))]
        return jnp.concatenate(parts, axis=1)

    def pack(x):
        return jnp.concatenate([x[:, :half], x[:, half:]], axis=0).astype(BF)

    m_s[...] = flip_cols(mm(jr, n_ref[1]).astype(BF))
    toks[0:2, :] = jnp.where(mask_ref[...] == 1, 5, ids_ref[...])
    hs[0] = pack(n_ref[0, rows - 16 :, :].astype(F32)[16 - PAD :])
    hs[1] = pack(m_s[0:16, :].astype(F32)[:PAD])
    hs[2] = pack(g_ref[0, 0:16, :].astype(F32)[:PAD])
    hs[3] = pack(flip_cols(mm(jr, g_ref[1]).astype(BF)).astype(F32)[rows - PAD :])
    same_prev, same_next = t_prev == c, t_next == c
    pl.semaphore_wait(
        barrier,
        2 * nf + 1 + jnp.where(same_prev, 0, 1) + jnp.where(same_next, 0, 1),
    )

    m_copy = rdma(m_s, m_r, m_sem, partner, f)
    m_copy.start()
    w_far = [
        rdma(proj_ref, w.at[f], w_sem.at[t], c, lax.rem(chip + t, nx) * 2 + core)
        for t in range(1, nx)
    ]
    w_near = rdma(proj_ref, w.at[f], w_sem.at[0], c, sib)
    for copy in w_far:
        copy.start()
    w_near.start()
    h_up = rdma(hs.at[0], hr.at[0], h_sem.at[0], up, f)
    h_down = rdma(hs.at[2], hr.at[2], h_sem.at[2], down, f)
    h_prev = rdma(hs.at[1], hr.at[1], h_sem.at[1], t_prev, f)
    h_next = rdma(hs.at[3], hr.at[3], h_sem.at[3], t_next, f)
    k_pair = rdma(toks, tokr.at[0], t_sem.at[0], partner, f)
    k_down = rdma(toks, tokr.at[1], t_sem.at[1], down, f)
    k_next = rdma(toks, tokr.at[2], t_sem.at[2], t_next, f)
    for copy in (h_up, h_down, k_pair, k_down):
        copy.start()

    @pl.when(same_prev)
    def _():
        hr[1] = hs[1]

    @pl.when(jnp.logical_not(same_prev))
    def _():
        h_prev.start()

    @pl.when(same_next)
    def _():
        hr[3] = hs[3]
        tokr[2] = toks[...]

    @pl.when(jnp.logical_not(same_next))
    def _():
        h_next.start()
        k_next.start()

    def order(j):
        return jnp.where(lax.rem(j, 2) == 0, j // 2, nc - 1 - j // 2)

    def order_py(j):
        return j // 2 if j % 2 == 0 else nc - 1 - j // 2

    g_copies = []
    for j in range(nc):
        q = order_py(j)
        src = g_ref[1, :, (nc - 1 - q) * cw : (nc - q) * cw]
        g1s[q] = mm(mm(jr, src).astype(BF), jc).astype(BF)
        g_copies.append(rdma(g1s.at[q], g1r.at[q], g_sem.at[q], partner, f))
        g_copies[-1].start()

    fb[...] = jnp.zeros_like(fb)
    fb[0, 0:taps, :] = filt_ref[...]
    fb[1, 0 : bias_ref.shape[0], :] = bias_ref[...]
    for q in range(nc):
        cols = slice(q * cw, (q + 1) * cw)
        ft[0, q] = fb[0, :, cols]
        ft[1, nc - 1 - q] = flip_f32(fb[0, :, cols], jc)
        for strand, at_q in ((0, q), (1, nc - 1 - q)):
            table = fb[1, :, cols] if strand == 0 else flip_f32(fb[1, :, cols], jc)
            hi, mid, _ = split3(table)
            gb[strand, at_q] = jnp.concatenate([hi.astype(F32), mid.astype(F32)], axis=0).astype(BF)
    both = [
        n_ref[0, :, :half],
        n_ref[1, :, :half],
        flip_cols(n_ref[0])[:, :half],
        m_s[:, :half],
    ]
    both[3] = mm(jr, both[3]).astype(BF)
    for i, part in enumerate(both):
        at[:, i * rows : (i + 1) * rows] = part.astype(F32).T.astype(BF)

    w[f] = proj_ref[...]
    w_pass = []
    for t in range(1, nx):
        w_far[t - 1].wait_recv()
        src_f = lax.rem(chip + nx - t, nx) * 2 + core
        w_pass.append(rdma(w.at[src_f], w.at[src_f], wf_sem.at[t - 1], c, sib))
        w_pass[-1].start()
    w_near.wait_recv()
    for copy in w_pass:
        copy.wait_recv()
    for r in range(nf):
        w[2 * nf - 1 - r] = flip_cols(mm(jr, w[r]).astype(BF))

    h_up.wait_recv()
    h_down.wait_recv()
    k_pair.wait_recv()
    k_down.wait_recv()

    @pl.when(jnp.logical_not(same_prev))
    def _():
        h_prev.wait_recv()

    @pl.when(jnp.logical_not(same_next))
    def _():
        h_next.wait_recv()
        k_next.wait_recv()

    def unpack(x):
        x = x.astype(F32)
        return jnp.concatenate([x[:PAD], x[PAD:]], axis=1)

    first, last = c == 0, c == n - 1
    nh0 = jnp.where(first, 0.0, unpack(hr[0]))
    nh1 = jnp.where(last, 0.0, unpack(hr[1]))
    rim = jnp.concatenate([nh0, nh1], axis=0).astype(BF)
    gt0 = jnp.where(last, 0.0, unpack(hr[2]))
    gt1 = jnp.where(first, 0.0, unpack(hr[3]))
    classes = lax.rem(lax.broadcasted_iota(jnp.int32, (16, rows), 0), 8)
    sources = (toks[0:1, :], tokr[1, 0:1, :], tokr[0, 1:2, :], tokr[2, 1:2, :])
    for i, row in enumerate(sources):
        hot = jnp.where(classes == row, 1.0, 0.0).astype(BF)
        turn = eye(rows) if i < 2 else jr
        oh[i] = mm_nt(turn, hot).astype(BF)
        oht[i] = mm(hot, turn).astype(BF)
    for q in range(nc):
        cols = slice(q * cw, (q + 1) * cw)
        gh0[q] = gt0[:, cols]
        gh1[q] = gt1[:, cols]
        wq = w[:, :, cols].reshape(width, cw)
        v0[q, PAD:, :] = mm(n_ref[0], wq).astype(BF).astype(F32)
        edge = mm(rim, wq).astype(BF).astype(F32)
        v0[q, 0:PAD, :] = edge[:PAD]
        v1[q, rows:, :] = edge[PAD:]
    m_copy.wait_recv()
    for q in range(nc):
        wq = w[:, :, q * cw : (q + 1) * cw].reshape(width, cw)
        v1[q, 0:rows, :] = mm(m_r[...], wq).astype(BF).astype(F32)

    def column_step(j, carry):
        q = order(j)
        back = nc - 1 - q
        rdma(g1s.at[q], g1r.at[q], g_sem.at[q], partner, f).wait_recv()
        off = pl.multiple_of(q * cw, cw)
        g0 = jnp.concatenate([g_ref[0, :, pl.ds(off, cw)].astype(F32), gh0[q]], axis=0)
        g1 = jnp.concatenate([gh1[q], g1r[q].astype(F32)], axis=0)
        b0 = jnp.concatenate([mm(oh[0], gb[0, q]), mm(oh[1], gb[0, q])[:PAD]], axis=0)
        b1 = jnp.concatenate([mm(oh[3], gb[1, q])[rows - PAD :], mm(oh[2], gb[1, q])], axis=0)
        gate0 = jax.nn.sigmoid(v1[q] + b0)
        gate1 = jax.nn.sigmoid(v0[q] + b1)
        cg0s[...] = g0 * gate0
        cg1s[...] = g1 * gate1
        cg0, cg1 = cg0s[0:rows, :], cg1s[PAD:, :]
        conv0 = jnp.zeros((rows, cw), F32)
        conv1 = jnp.zeros((rows, cw), F32)
        for k in range(taps):
            a0 = v0[q, PAD - k : PAD - k + rows, :]
            a1 = v1[q, k : k + rows, :]
            conv0 = conv0 + ft[0, q, k : k + 1, :] * a0
            conv1 = conv1 + ft[1, q, k : k + 1, :] * a1
            s0[q, k : k + 1, :] = jnp.sum(cg0 * a0, axis=0, keepdims=True) * scale
            s1[back, k : k + 1, :] = jnp.sum(cg1 * a1, axis=0, keepdims=True) * scale
        s0[q, taps:8, :] = jnp.zeros((8 - taps, cw), F32)
        s1[back, taps:8, :] = jnp.zeros((8 - taps, cw), F32)
        gp0 = cg0 * conv0 * (1.0 - gate0[:rows])
        gp1 = cg1 * conv1 * (1.0 - gate1[PAD:])
        for store, at_q, hot, gp in ((s0, q, oht[0], gp0), (s1, back, oht[2], gp1)):
            hi, mid, _ = split3(gp)
            store[at_q, 8:16, :] = (mm(hot, hi) + mm(hot, mid))[:8] * scale
        s1[back] = flip_f32(s1[back], jc)
        vga = gp1.astype(BF).astype(F32)
        vgb = gp0.astype(BF).astype(F32)
        for k in range(taps):
            vga = vga + ft[0, q, k : k + 1, :] * cg0s[k : k + rows, :]
            vgb = vgb + ft[1, q, k : k + 1, :] * cg1s[PAD - k : PAD - k + rows, :]
        vg0[q] = vga.astype(BF)
        vgs[back] = mm(mm(jr, vgb.astype(BF)).astype(BF), jc).astype(BF)
        rdma(vgs.at[back], vgr.at[back], vg_sem.at[back], partner, f).start()
        return carry

    lax.fori_loop(0, nc, column_step, 0)

    small = []
    for t in range(nf):
        other = lax.rem(f + t, nf)
        small.append(rdma(s1.at[other], sr.at[1, t], s1_sem.at[t], partner, other))
        if t > 0:
            small.append(rdma(s0.at[other], sr.at[0, t], s0_sem.at[t], c, other))
    for copy in small:
        copy.start()

    def vg_wait(q):
        rdma(vgs.at[q], vgr.at[q], vg_sem.at[q], partner, f).wait_recv()

    def weight_part(p):
        lo, hi = p, nc - 1 - p
        vg_wait(hi)
        vg_wait(lo)
        for i, (a, b) in enumerate(((lo, hi), (hi, lo))):
            right = jnp.concatenate(
                [vg0[a], vgr[a], mm(vg0[b], jc).astype(BF), mm(vgr[b], jc).astype(BF)], axis=0
            )
            pf[p, i] = (mm(at[...], right) * scale).reshape(nf, half // nf, cw)
            for x in range(nx):
                cs[p, i * nx + x] = pf[p, i, 2 * x + 1 - core].astype(BF)
        copy = rdma(cs.at[p], cr.at[p], c_sem.at[p], c, sib)
        copy.start()
        return copy

    def weight_pass(p, copy):
        copy.wait_recv()
        out = []
        for t in range(1, nx):
            xt = lax.rem(chip + t, nx)
            for i in range(2):
                xs[p, t - 1, i] = (pf[p, i, 2 * xt + core] + cr[p, i * nx + xt].astype(F32)).astype(BF)
            out.append(rdma(xs.at[p, t - 1], xr.at[p, t - 1], x_sem.at[p, t - 1], c, 2 * xt + core))
            out[-1].start()
        return out

    def weight_end(p, copies):
        for copy in copies:
            copy.wait_recv()
        for i, q in enumerate((p, nc - 1 - p)):
            total = pf[p, i, f] + cr[p, i * nx + chip].astype(F32)
            for t in range(1, nx):
                total = total + xr[p, t - 1, i].astype(F32)
            proj_out[0, :, q * cw : (q + 1) * cw] = total

    def grad_in(strand, blocks):
        full = jnp.concatenate([blocks[q] for q in range(nc)], axis=1)
        for r in range(nf):
            wr = w[2 * r : 2 * r + 2].reshape(2 * w.shape[1], width)
            in_out[strand, :, r * wr.shape[0] : (r + 1) * wr.shape[0]] = mm_nt(full, wr).astype(BF)

    cores, crosses = [], []
    for p in range(nc // 2):
        cores.append(weight_part(p))
        if p == 0:
            grad_in(0, vg0)
        if p == nc // 2 - 1:
            grad_in(1, vgr)
        crosses.append(weight_pass(p, cores[p]))

    for copy in small:
        copy.wait_recv()
    total = s0[f] + sr[1, 0]
    for t in range(1, nf):
        total = total + sr[0, t] + sr[1, t]
    filt_out[0] = total[0:taps, :]
    bias_out[0] = total[8 : 8 + bias_out.shape[1], :]
    for p in range(nc // 2):
        weight_end(p, crosses[p])

    m_copy.wait_send()
    for copy in w_far + [w_near] + w_pass + [h_up, h_down, k_pair, k_down] + g_copies + small + cores:
        copy.wait_send()
    for copies in crosses:
        for copy in copies:
            copy.wait_send()
    for q in range(nc):
        rdma(vgs.at[q], vgr.at[q], vg_sem.at[q], partner, f).wait_send()

    @pl.when(jnp.logical_not(same_prev))
    def _():
        h_prev.wait_send()

    @pl.when(jnp.logical_not(same_next))
    def _():
        h_next.wait_send()
        k_next.wait_send()


def shards(n, nf, normed, out_grad, ids, mask, proj_half, conv_filter, gate_bias):
    _, seq_local, rows, width = normed.shape
    assert seq_local == 1
    taps, kinds = conv_filter.shape[0], gate_bias.shape[0]
    nc, cw, nx = nf, width // nf, nf // 2
    share = proj_half.shape[0]
    ext = rows + PAD
    scale = 1.0 / math.sqrt(2.0 * seq_local * nf * rows)
    vm = pltpu.VMEM
    dma = pltpu.SemaphoreType.DMA
    scratch = [
        vm((rows, width), BF), vm((rows, width), BF),
        vm((nc, rows, cw), BF), vm((nc, rows, cw), BF),
        vm((nc, rows, cw), BF), vm((nc, rows, cw), BF), vm((nc, rows, cw), BF),
        vm((4, 2 * PAD, width // 2), BF), vm((4, 2 * PAD, width // 2), BF),
        vm((8, rows), jnp.int32), vm((3, 8, rows), jnp.int32),
        vm((2 * nf, share, width), BF),
        vm((nc, ext, cw), F32), vm((nc, ext, cw), F32),
        vm((ext, cw), F32), vm((ext, cw), F32),
        vm((nc, PAD, cw), F32), vm((nc, PAD, cw), F32),
        vm((4, rows, 16), BF), vm((4, 16, rows), BF),
        vm((2, nc, 16, cw), BF), vm((2, nc, 8, cw), F32), vm((2, 8, width), F32),
        vm((nf, 16, cw), F32), vm((nf, 16, cw), F32), vm((2, nf, 16, cw), F32),
        vm((width // 2, 4 * rows), BF),
        vm((nc // 2, 2, nf, share, cw), F32),
        vm((nc // 2, 2 * nx, share, cw), BF), vm((nc // 2, 2 * nx, share, cw), BF),
        vm((nc // 2, nx - 1, 2, share, cw), BF), vm((nc // 2, nx - 1, 2, share, cw), BF),
        dma((2,)), dma((nc, 2)), dma((nc, 2)), dma((4, 2)), dma((3, 2)), dma((nx, 2)),
        dma((nx - 1, 2)), dma((nf, 2)), dma((nf, 2)), dma((nc // 2, 2)), dma((nc // 2, nx - 1, 2)),
    ]
    in_grad, proj, filt, bias = pl.pallas_call(
        functools.partial(kernel, n, nf, taps, scale),
        out_shape=(
            jax.ShapeDtypeStruct((2, rows, width), BF),
            jax.ShapeDtypeStruct((1, share, width), F32),
            jax.ShapeDtypeStruct((1, taps, cw), F32),
            jax.ShapeDtypeStruct((1, kinds, cw), F32),
        ),
        in_specs=[pl.BlockSpec(memory_space=pltpu.VMEM)] * 7,
        out_specs=[pl.BlockSpec(memory_space=pltpu.VMEM)] * 4,
        scratch_shapes=scratch,
        compiler_params=pltpu.CompilerParams(
            collective_id=0, has_side_effects=True, vmem_limit_bytes=48 * 1024 * 1024
        ),
    )(
        normed.reshape(2, rows, width),
        out_grad.reshape(2, rows, width),
        ids.reshape(2, rows),
        mask.reshape(2, rows),
        proj_half,
        conv_filter,
        gate_bias,
    )
    return in_grad.reshape(normed.shape), proj, filt, bias


def solution(mesh):
    placed = (
        P(None, "fsdp", "ctx", None),
        P(None, "fsdp", "ctx", None),
        P(None, "fsdp", "ctx"),
        P(None, "fsdp", "ctx"),
        P("fsdp", None),
        P(),
        P(),
    )
    return jax.shard_map(
        functools.partial(shards, mesh.shape["ctx"], mesh.shape["fsdp"]),
        mesh=mesh,
        in_specs=placed,
        out_specs=(
            P(None, "fsdp", "ctx", None),
            P("ctx", "fsdp", None),
            P("ctx", None, "fsdp"),
            P("ctx", None, "fsdp"),
        ),
        check_vma=False,
    )
```

time: 206 us -> 64.7 us (0.31)
  the two profiles are of different devices: /device:TPU:0 before, /device:TPU:15 now
where the time goes in v1:
time: 64.7 us; the launch traced here: 64.3 us
  Pallas kernels  55.6 us (86%)
  local copies, waits for them, and re-layouts  8.01 us (12%)
  between operations  0.66 us (1%)
    pallas_call x1, Pallas kernels, shards(): pl.pallas_call(functools.partial(kernel, n, nf, taps, scale), out_shape=(...  55.6 us
    unnamed x18, local copies, waits for them, and re-layouts  8.01 us

profile of v1, /device:TPU:15, one launch (start us, length us, event | category | flops | bytes accessed | tf_op | source)
XLA Modules:
  0.0 64.3 jit_solution(4810034427506980929)
XLA Ops:
  0.6 0.0 copy-start.6
  0.6 0.0 copy-start.5
  0.7 0.7 %copy-done.6 = s32[2,1,128]{2,1,0:T(1,128)S(1)} copy-done((s32[2,1,128]{2,1,0:T(1,128)S(1)}, s32[2,1,128]{2,1,0:T(1,128)}, u32[]{:S(2)}) %copy-start.6) | copy-done | bytes 1048
  1.3 0.0 copy-done.5
  1.3 0.0 copy-start
  1.3 1.0 %copy-done = bf16[2,1,128,1024]{3,2,1,0:T(8,128)(2,1)S(1)} copy-done((bf16[2,1,128,1024]{3,2,1,0:T(8,128)(2,1)S(1)}, bf16[2,1,128,1024]{3,2,1,0:T(8,128)(2,1)}, u32[]{:S(2)}) %copy-start) | copy-done | bytes 524312
  2.4 0.0 copy-start.1
  2.4 1.0 %copy-done.1 = bf16[2,1,128,1024]{3,2,1,0:T(8,128)(2,1)S(1)} copy-done((bf16[2,1,128,1024]{3,2,1,0:T(8,128)(2,1)S(1)}, bf16[2,1,128,1024]{3,2,1,0:T(8,128)(2,1)}, u32[]{:S(2)}) %copy-start.1) | copy-done | bytes 524312
  3.4 0.0 copy-start.2
  3.4 0.9 %copy-done.2 = bf16[128,1024]{1,0:T(8,128)(2,1)S(1)} copy-done((bf16[128,1024]{1,0:T(8,128)(2,1)S(1)}, bf16[128,1024]{1,0:T(8,128)(2,1)}, u32[]{:S(2)}) %copy-start.2) | copy-done | bytes 262168
  4.4 0.0 copy-start.3
  4.4 0.8 %copy-done.3 = f32[7,1024]{1,0:T(8,128)S(1)} copy-done((f32[7,1024]{1,0:T(8,128)S(1)}, f32[7,1024]{1,0:T(8,128)}, u32[]{:S(2)}) %copy-start.3) | copy-done | bytes 28696
  5.1 0.0 copy-start.4
  5.1 0.8 %copy-done.4 = f32[6,1024]{1,0:T(8,128)S(1)} copy-done((f32[6,1024]{1,0:T(8,128)S(1)}, f32[6,1024]{1,0:T(8,128)}, u32[]{:S(2)}) %copy-start.4) | copy-done | bytes 24600
  5.9 55.6 %shard_map.102 = (bf16[2,128,1024]{2,1,0:T(8,128)(2,1)S(1)}, f32[1,128,1024]{2,1,0:T(8,128)S(1)}, f32[1,7,256]{2,1,0:T(8,128)S(1)}, f32[1,6,256]{2,1,0:T(8,128)S(1)}) custom-call(bf16[2,128,1024]{2,1,0:T(8,128)(2,1)S(1)} %bitcast.7, bf16[2,128,1024]{2,1,0:T(8,128)(2,1)S(1)} %bitcast.8, s32[2,128]{1,0:T(2,128)S(1)} %bitcast.10, s32[2,128]{1,0:T(2,128)S(1)} %bitcast.11, ...), custom_call_target="tpu_custom_call" | custom-call | tf_op jit(solution)/shard_map/pallas_call | solution.py:410
  61.5 0.6 copy.13
  62.1 0.6 copy.12
  62.7 0.8 %copy.16 = bf16[2,1,128,1024]{3,2,1,0:T(8,128)(2,1)} copy(bf16[2,1,128,1024]{3,2,1,0:T(8,128)(2,1)S(1)} %bitcast.9) | data formatting | bytes 1048576
  63.5 0.8 %copy.17 = f32[1,128,1024]{2,1,0:T(8,128)} copy(f32[1,128,1024]{2,1,0:T(8,128)S(1)} %get-tuple-element.21) | data formatting | bytes 1048576
Async XLA Ops:
  0.6 0.7 %copy-start.6 = (s32[2,1,128]{2,1,0:T(1,128)S(1)}, s32[2,1,128]{2,1,0:T(1,128)}, u32[]{:S(2)}) copy-start(s32[2,1,128]{2,1,0:T(1,128)} %param.10) | copy-start | bytes 3076
  0.6 0.7 %copy-start.5 = (s32[2,1,128]{2,1,0:T(1,128)S(1)}, s32[2,1,128]{2,1,0:T(1,128)}, u32[]{:S(2)}) copy-start(s32[2,1,128]{2,1,0:T(1,128)} %param.9) | copy-start | bytes 3076
  1.3 1.0 %copy-start = (bf16[2,1,128,1024]{3,2,1,0:T(8,128)(2,1)S(1)}, bf16[2,1,128,1024]{3,2,1,0:T(8,128)(2,1)}, u32[]{:S(2)}) copy-start(bf16[2,1,128,1024]{3,2,1,0:T(8,128)(2,1)} %param.7) | copy-start | bytes 1572868
  2.4 1.0 %copy-start.1 = (bf16[2,1,128,1024]{3,2,1,0:T(8,128)(2,1)S(1)}, bf16[2,1,128,1024]{3,2,1,0:T(8,128)(2,1)}, u32[]{:S(2)}) copy-start(bf16[2,1,128,1024]{3,2,1,0:T(8,128)(2,1)} %param.8) | copy-start | bytes 1572868
  3.4 0.9 %copy-start.2 = (bf16[128,1024]{1,0:T(8,128)(2,1)S(1)}, bf16[128,1024]{1,0:T(8,128)(2,1)}, u32[]{:S(2)}) copy-start(bf16[128,1024]{1,0:T(8,128)(2,1)} %proj_ref.1) | copy-start | bytes 786436
  4.4 0.8 %copy-start.3 = (f32[7,1024]{1,0:T(8,128)S(1)}, f32[7,1024]{1,0:T(8,128)}, u32[]{:S(2)}) copy-start(f32[7,1024]{1,0:T(8,128)} %filt_ref.1) | copy-start | bytes 86020
  5.1 0.8 %copy-start.4 = (f32[6,1024]{1,0:T(8,128)S(1)}, f32[6,1024]{1,0:T(8,128)}, u32[]{:S(2)}) copy-start(f32[6,1024]{1,0:T(8,128)} %bias_ref.1) | copy-start | bytes 73732

commit v2 on v1

--- a/solution.py
+++ b/solution.py
@@ -49,11 +49,12 @@
 
 def kernel(
     n, nf, taps, scale,
-    n_ref, g_ref, ids_ref, mask_ref, proj_ref, filt_ref, bias_ref,
+    n_hbm, g_hbm, ids_hbm, mask_hbm, proj_ref, filt_hbm, bias_hbm,
     in_out, proj_out, filt_out, bias_out,
+    n_ref, g_ref, ids_ref, mask_ref, filt_ref, bias_ref, s1t, s1r,
     m_s, m_r, g1s, g1r, vgs, vgr, vg0, hs, hr, toks, tokr, w, v0, v1, cg0s, cg1s,
     gh0, gh1, oh, oht, gb, ft, fb, s0, s1, sr, at, pf, cs, cr, xs, xr,
-    m_sem, g_sem, vg_sem, h_sem, t_sem, w_sem, wf_sem, s0_sem, s1_sem, c_sem, x_sem,
+    in_sem, s1t_sem, m_sem, g_sem, vg_sem, h_sem, t_sem, w_sem, wf_sem, s0_sem, s1_sem, c_sem, x_sem,
 ):
     rows, width = m_s.shape
     nc, _, cw = g1s.shape
@@ -74,6 +75,24 @@
             device_id=(cc, ff), device_id_type=MESH,
         )
 
+    loads = [
+        pltpu.make_async_copy(src, dst, in_sem.at[i])
+        for i, (src, dst) in enumerate(
+            (
+                (n_hbm.at[1], n_ref.at[1]),
+                (g_hbm.at[1], g_ref.at[1]),
+                (ids_hbm, ids_ref),
+                (mask_hbm, mask_ref),
+                (n_hbm.at[0], n_ref.at[0]),
+                (g_hbm.at[0], g_ref.at[0]),
+                (filt_hbm, filt_ref),
+                (bias_hbm, bias_ref),
+                (proj_ref, w.at[f]),
+            )
+        )
+    ]
+    for load in loads:
+        load.start()
     barrier = pltpu.get_barrier_semaphore()
 
     def greet(cc, ff):
@@ -100,12 +119,8 @@
     def pack(x):
         return jnp.concatenate([x[:, :half], x[:, half:]], axis=0).astype(BF)
 
+    loads[0].wait()
     m_s[...] = flip_cols(mm(jr, n_ref[1]).astype(BF))
-    toks[0:2, :] = jnp.where(mask_ref[...] == 1, 5, ids_ref[...])
-    hs[0] = pack(n_ref[0, rows - 16 :, :].astype(F32)[16 - PAD :])
-    hs[1] = pack(m_s[0:16, :].astype(F32)[:PAD])
-    hs[2] = pack(g_ref[0, 0:16, :].astype(F32)[:PAD])
-    hs[3] = pack(flip_cols(mm(jr, g_ref[1]).astype(BF)).astype(F32)[rows - PAD :])
     same_prev, same_next = t_prev == c, t_next == c
     pl.semaphore_wait(
         barrier,
@@ -122,6 +137,14 @@
     for copy in w_far:
         copy.start()
     w_near.start()
+    for load in loads[1:]:
+        load.wait()
+    for i in range(2):
+        toks[i : i + 1, :] = jnp.where(mask_ref[i] == 1, 5, ids_ref[i])
+    hs[0] = pack(n_ref[0, rows - 16 :, :].astype(F32)[16 - PAD :])
+    hs[1] = pack(m_s[0:16, :].astype(F32)[:PAD])
+    hs[2] = pack(g_ref[0, 0:16, :].astype(F32)[:PAD])
+    hs[3] = pack(flip_cols(mm(anti(16), g_ref[1, 0:16, :]).astype(BF)).astype(F32)[16 - PAD :])
     h_up = rdma(hs.at[0], hr.at[0], h_sem.at[0], up, f)
     h_down = rdma(hs.at[2], hr.at[2], h_sem.at[2], down, f)
     h_prev = rdma(hs.at[1], hr.at[1], h_sem.at[1], t_prev, f)
@@ -185,7 +208,6 @@
     for i, part in enumerate(both):
         at[:, i * rows : (i + 1) * rows] = part.astype(F32).T.astype(BF)
 
-    w[f] = proj_ref[...]
     w_pass = []
     for t in range(1, nx):
         w_far[t - 1].wait_recv()
@@ -287,11 +309,10 @@
     lax.fori_loop(0, nc, column_step, 0)
 
     small = []
-    for t in range(nf):
+    for t in range(1, nf):
         other = lax.rem(f + t, nf)
-        small.append(rdma(s1.at[other], sr.at[1, t], s1_sem.at[t], partner, other))
-        if t > 0:
-            small.append(rdma(s0.at[other], sr.at[0, t], s0_sem.at[t], c, other))
+        small.append(rdma(s1.at[other], sr.at[1, t], s1_sem.at[t], c, other))
+        small.append(rdma(s0.at[other], sr.at[0, t], s0_sem.at[t], c, other))
     for copy in small:
         copy.start()
 
@@ -339,26 +360,32 @@
             wr = w[2 * r : 2 * r + 2].reshape(2 * w.shape[1], width)
             in_out[strand, :, r * wr.shape[0] : (r + 1) * wr.shape[0]] = mm_nt(full, wr).astype(BF)
 
+    grad_in(0, vg0)
+    for copy in small:
+        copy.wait_recv()
+    total, across = s0[f], s1[f]
+    for t in range(1, nf):
+        total = total + sr[0, t]
+        across = across + sr[1, t]
+    s1t[...] = across
+    s1_copy = rdma(s1t, s1r, s1t_sem, partner, f)
+    s1_copy.start()
     cores, crosses = [], []
     for p in range(nc // 2):
         cores.append(weight_part(p))
-        if p == 0:
-            grad_in(0, vg0)
         if p == nc // 2 - 1:
             grad_in(1, vgr)
         crosses.append(weight_pass(p, cores[p]))
 
-    for copy in small:
-        copy.wait_recv()
-    total = s0[f] + sr[1, 0]
-    for t in range(1, nf):
-        total = total + sr[0, t] + sr[1, t]
+    s1_copy.wait_recv()
+    total = total + s1r[...]
     filt_out[0] = total[0:taps, :]
     bias_out[0] = total[8 : 8 + bias_out.shape[1], :]
     for p in range(nc // 2):
         weight_end(p, crosses[p])
 
     m_copy.wait_send()
+    s1_copy.wait_send()
     for copy in w_far + [w_near] + w_pass + [h_up, h_down, k_pair, k_down] + g_copies + small + cores:
         copy.wait_send()
     for copies in crosses:
@@ -388,6 +415,10 @@
     vm = pltpu.VMEM
     dma = pltpu.SemaphoreType.DMA
     scratch = [
+        vm((2, rows, width), BF), vm((2, rows, width), BF),
+        vm((2, 1, rows), jnp.int32), vm((2, 1, rows), jnp.int32),
+        vm((taps, width), F32), vm((kinds, width), F32),
+        vm((16, cw), F32), vm((16, cw), F32),
         vm((rows, width), BF), vm((rows, width), BF),
         vm((nc, rows, cw), BF), vm((nc, rows, cw), BF),
         vm((nc, rows, cw), BF), vm((nc, rows, cw), BF), vm((nc, rows, cw), BF),
@@ -404,7 +435,7 @@
         vm((nc // 2, 2, nf, share, cw), F32),
         vm((nc // 2, 2 * nx, share, cw), BF), vm((nc // 2, 2 * nx, share, cw), BF),
         vm((nc // 2, nx - 1, 2, share, cw), BF), vm((nc // 2, nx - 1, 2, share, cw), BF),
-        dma((2,)), dma((nc, 2)), dma((nc, 2)), dma((4, 2)), dma((3, 2)), dma((nx, 2)),
+        dma((9,)), dma((2,)), dma((2,)), dma((nc, 2)), dma((nc, 2)), dma((4, 2)), dma((3, 2)), dma((nx, 2)),
         dma((nx - 1, 2)), dma((nf, 2)), dma((nf, 2)), dma((nc // 2, 2)), dma((nc // 2, nx - 1, 2)),
     ]
     in_grad, proj, filt, bias = pl.pallas_call(
@@ -415,17 +446,17 @@
             jax.ShapeDtypeStruct((1, taps, cw), F32),
             jax.ShapeDtypeStruct((1, kinds, cw), F32),
         ),
-        in_specs=[pl.BlockSpec(memory_space=pltpu.VMEM)] * 7,
+        in_specs=[pl.BlockSpec(memory_space=pltpu.HBM)] * 7,
         out_specs=[pl.BlockSpec(memory_space=pltpu.VMEM)] * 4,
         scratch_shapes=scratch,
         compiler_params=pltpu.CompilerParams(
-            collective_id=0, has_side_effects=True, vmem_limit_bytes=48 * 1024 * 1024
+            collective_id=0, has_side_effects=True, vmem_limit_bytes=56 * 1024 * 1024
         ),
     )(
         normed.reshape(2, rows, width),
         out_grad.reshape(2, rows, width),
-        ids.reshape(2, rows),
-        mask.reshape(2, rows),
+        ids,
+        mask,
         proj_half,
         conv_filter,
         gate_bias,

time: 64.7 us -> 59.4 us (0.918)
  local copies, waits for them, and re-layouts: 8.01 us -> 4.61 us
  Pallas kernels: 55.6 us -> 53.9 us
    unnamed x18 -> x10, local copies, waits for them, and re-layouts: 8.01 us -> 4.61 us
    pallas_call x1, Pallas kernels: 55.6 us -> 53.9 us  [shards(): pl.pallas_call(functools.partial(kernel, n, nf, taps, scale), out_shape=(...]
where the time goes in v2:
time: 59.4 us; the launch traced here: 59.2 us
  Pallas kernels  53.9 us (91%)
  local copies, waits for them, and re-layouts  4.61 us (8%)
  between operations  0.66 us (1%)
    pallas_call x1, Pallas kernels, shards(): pl.pallas_call(functools.partial(kernel, n, nf, taps, scale), out_shape=(...  53.9 us
    unnamed x10, local copies, waits for them, and re-layouts  4.61 us

profile of v2, /device:TPU:15, one launch (start us, length us, event | category | flops | bytes accessed | tf_op | source)
XLA Modules:
  0.0 59.2 jit_solution(7915562004957679451)
XLA Ops:
  0.6 53.9 %shard_map.102 = (bf16[2,128,1024]{2,1,0:T(8,128)(2,1)}, f32[1,128,1024]{2,1,0:T(8,128)}, f32[1,7,256]{2,1,0:T(8,128)}, f32[1,6,256]{2,1,0:T(8,128)}) custom-call(bf16[2,128,1024]{2,1,0:T(8,128)(2,1)} %bitcast.5, bf16[2,128,1024]{2,1,0:T(8,128)(2,1)} %bitcast.6, s32[2,1,128]{2,1,0:T(1,128)} %ids_hbm.1, s32[2,1,128]{2,1,0:T(1,128)} %mask_hbm.1, ...), custom_call_target="tpu_custom_call" | custom-call | tf_op jit(solution)/shard_map/pallas_call | solution.py:441
  54.6 0.0 copy-start.1
  54.6 0.0 copy-start.2
  54.6 0.7 %copy-done.1 = f32[1,6,256]{2,1,0:T(8,128)S(1)} copy-done((f32[1,6,256]{2,1,0:T(8,128)S(1)}, f32[1,6,256]{2,1,0:T(8,128)}, u32[]{:S(2)}) %copy-start.1) | copy-done | bytes 6168
  55.3 0.6 %copy.13 = f32[1,6,256]{2,0,1:T(1,128)} copy(f32[1,6,256]{2,1,0:T(8,128)S(1)} %copy-done.1) | data formatting | bytes 12288
  55.9 0.0 copy-done.2
  55.9 0.6 %copy.12 = f32[1,7,256]{2,0,1:T(1,128)} copy(f32[1,7,256]{2,1,0:T(8,128)S(1)} %copy-done.2) | data formatting | bytes 14336
  56.5 0.0 copy-start
  56.5 1.9 %copy.16 = bf16[2,1,128,1024]{3,2,1,0:T(8,128)(2,1)} copy(bf16[2,1,128,1024]{3,2,1,0:T(8,128)(2,1)} %bitcast.7) | data formatting | bytes 1048576
  58.4 0.0 copy-done
  58.4 0.8 %copy.17 = f32[1,128,1024]{2,1,0:T(8,128)} copy(f32[1,128,1024]{2,1,0:T(8,128)S(1)} %copy-done) | data formatting | bytes 1048576
Async XLA Ops:
  54.6 0.7 %copy-start.1 = (f32[1,6,256]{2,1,0:T(8,128)S(1)}, f32[1,6,256]{2,1,0:T(8,128)}, u32[]{:S(2)}) copy-start(f32[1,6,256]{2,1,0:T(8,128)} %get-tuple-element.15) | copy-start | bytes 18436
  54.6 1.3 %copy-start.2 = (f32[1,7,256]{2,1,0:T(8,128)S(1)}, f32[1,7,256]{2,1,0:T(8,128)}, u32[]{:S(2)}) copy-start(f32[1,7,256]{2,1,0:T(8,128)} %get-tuple-element.14) | copy-start | bytes 21508
  56.5 1.9 %copy-start = (f32[1,128,1024]{2,1,0:T(8,128)S(1)}, f32[1,128,1024]{2,1,0:T(8,128)}, u32[]{:S(2)}) copy-start(f32[1,128,1024]{2,1,0:T(8,128)} %get-tuple-element.21) | copy-start | bytes 1572868
